TPU v7x, 32 devices: a whole 2x2x4 slice. The times are simulated.
32 devices in a mesh: tr: 4 (over x, core), gz: 8 (over z, y).
Axes of the slice: x: 2, y: 2, z: 4, core: 2. Of those that a mesh axis runs over, the one named last changes fastest.
Arguments:
- tokens: bfloat16 [40, 32, 8, 768], P('gz', None, 'tr'), may hold values from -6 to 6
- cotangent: bfloat16 [40, 32, 8, 768], P('gz', None, 'tr'), may hold values from -6 to 6
- gain_x: float32 [768], replicated, may hold values from 0.1 to 1.9
- wqkv_x: bfloat16 [768, 2304], P('tr'), as said below
- wo_x: bfloat16 [768, 768], P('tr'), may hold values from -0.21875 to 0.21875
- gain_z: float32 [768], replicated, may hold values from 0.1 to 1.9
- wqkv_z: bfloat16 [768, 2304], P('tr'), as said below
- wo_z: bfloat16 [768, 768], P('tr'), may hold values from -0.21875 to 0.21875
Outputs:
- grad_tokens: bfloat16 [40, 32, 8, 768], P('gz', None, 'tr')
Inputs may be any that keep to these rules, and one draw needn't show every extreme that they name: `wqkv_x`: query, key and value columns side by side, each block split into 6 heads of 128. `wqkv_z`: query, key and value columns side by side, each block split into 6 heads of 128.
All inputs are finite; a program needn't handle non-finite values.
Results may differ from a plain program's by a relative error of at most 0.038.
The roundings to bfloat16 on the way count: a program that leaves them out, or rounds other values in their place, can miss the bound.
Values may be sent and summed in bfloat16 or wider, within the bound.
A program may use at most 64 MiB of HBM per device.

v0:
```python
import math
import jax
import jax.numpy as jnp
from jax import lax
from jax.sharding import PartitionSpec as P

H = 6


def head_split(packed, index, model_width):
    piece = packed[..., index * model_width : (index + 1) * model_width]
    return piece.reshape(piece.shape[:-1] + (H, model_width // H))


def merge_heads(value):
    return value.reshape(value.shape[:-2] + (value.shape[-2] * value.shape[-1],))


def recompute(tokens_in, gain_vec, w_in, layout):
    model_width = w_in.shape[0]
    factor = 1.0 / math.sqrt(model_width // H)
    widened = tokens_in.astype(jnp.float32)
    inv_rms = lax.rsqrt(jnp.mean(widened * widened, axis=-1, keepdims=True) + 1e-06)
    normed = (widened * inv_rms * gain_vec).astype(jnp.bfloat16)
    packed = jnp.dot(normed, w_in, preferred_element_type=jnp.float32).astype(jnp.bfloat16)
    queries = head_split(packed, 0, model_width)
    key_part = head_split(packed, 1, model_width)
    values = head_split(packed, 2, model_width)
    key_form = layout.replace("l", "m")
    scores = (
        jnp.einsum(
            layout + "," + key_form + "->bhlm",
            queries,
            key_part,
            preferred_element_type=jnp.float32,
        )
        * factor
    )
    highest = jnp.max(scores, axis=-1, keepdims=True)
    expanded = jnp.exp(scores - highest)
    probs = expanded / jnp.sum(expanded, axis=-1, keepdims=True)
    return (widened, inv_rms, queries, key_part, values, probs, probs.astype(jnp.bfloat16), factor)


def forward_out(tokens_in, gain_vec, w_in, w_out, layout):
    widened, inv_rms, queries, key_part, values, probs, probs_b, factor = recompute(
        tokens_in, gain_vec, w_in, layout
    )
    key_form = layout.replace("l", "m")
    mixed = jnp.einsum(
        "bhlm," + key_form + "->" + layout, probs_b, values, preferred_element_type=jnp.float32
    )
    mixed = merge_heads(mixed.astype(jnp.bfloat16))
    return (widened + jnp.dot(mixed, w_out, preferred_element_type=jnp.float32)).astype(
        jnp.bfloat16
    )


def backward(tokens_in, upstream, gain_vec, w_in, w_out, layout):
    widened, inv_rms, queries, key_part, values, probs, probs_b, factor = recompute(
        tokens_in, gain_vec, w_in, layout
    )
    key_form = layout.replace("l", "m")
    d_mixed = jnp.dot(upstream, w_out.T, preferred_element_type=jnp.float32).astype(jnp.bfloat16)
    d_mixed = d_mixed.reshape(d_mixed.shape[:-1] + (H, d_mixed.shape[-1] // H))
    d_probs = jnp.einsum(
        layout + "," + key_form + "->bhlm", d_mixed, values, preferred_element_type=jnp.float32
    )
    d_values = jnp.einsum(
        "bhlm," + layout + "->" + key_form, probs_b, d_mixed, preferred_element_type=jnp.float32
    ).astype(jnp.bfloat16)
    centre = jnp.sum(probs * d_probs, axis=-1, keepdims=True)
    d_scores = (probs * (d_probs - centre) * factor).astype(jnp.bfloat16)
    d_queries = jnp.einsum(
        "bhlm," + key_form + "->" + layout, d_scores, key_part, preferred_element_type=jnp.float32
    ).astype(jnp.bfloat16)
    d_keys = jnp.einsum(
        "bhlm," + layout + "->" + key_form, d_scores, queries, preferred_element_type=jnp.float32
    ).astype(jnp.bfloat16)
    joined = jnp.concatenate(
        [merge_heads(d_queries), merge_heads(d_keys), merge_heads(d_values)], axis=-1
    )
    d_normed = jnp.dot(joined, w_in.T, preferred_element_type=jnp.float32)
    scaled = d_normed * gain_vec
    d_tokens = inv_rms * (
        scaled - widened * inv_rms * inv_rms * jnp.mean(scaled * widened, axis=-1, keepdims=True)
    )
    return (upstream.astype(jnp.float32) + d_tokens).astype(jnp.bfloat16)


def line_forward(lines, gain_vec, w_in, w_out):
    feature_count = lines.shape[3]
    flat = lines.reshape(-1, lines.shape[2], feature_count)
    return forward_out(flat, gain_vec, w_in, w_out, "blhe").reshape(lines.shape)


def line_backward(lines, upstream, gain_vec, w_in, w_out):
    feature_count = lines.shape[3]
    flat = lines.reshape(-1, lines.shape[2], feature_count)
    flat_up = upstream.reshape(flat.shape)
    return backward(flat, flat_up, gain_vec, w_in, w_out, "blhe").reshape(lines.shape)


def per_device(tokens, cotangent, gain_x, wqkv_x, wo_x, gain_z, wqkv_z, wo_z):
    full_in_x, full_out_x = (
        lax.all_gather(wqkv_x, "tr", axis=0, tiled=True),
        lax.all_gather(wo_x, "tr", axis=0, tiled=True),
    )
    full_in_z, full_out_z = (
        lax.all_gather(wqkv_z, "tr", axis=0, tiled=True),
        lax.all_gather(wo_z, "tr", axis=0, tiled=True),
    )
    width = tokens.shape[-1]
    lines = lax.all_to_all(tokens, "tr", split_axis=1, concat_axis=2, tiled=True)
    cot_lines = lax.all_to_all(cotangent, "tr", split_axis=1, concat_axis=2, tiled=True)
    cells = lines.shape[1] * lines.shape[2]
    flat = (lines.shape[0], cells, width)
    cot_columns = lax.all_to_all(
        cot_lines.reshape(flat), "gz", split_axis=1, concat_axis=0, tiled=True
    )
    mid_lines = line_forward(lines, gain_x, full_in_x, full_out_x)
    mid_columns = lax.all_to_all(
        mid_lines.reshape(flat), "gz", split_axis=1, concat_axis=0, tiled=True
    )
    grad_columns = backward(mid_columns, cot_columns, gain_z, full_in_z, full_out_z, "lbhe")
    grad_lines = lax.all_to_all(grad_columns, "gz", split_axis=0, concat_axis=1, tiled=True)
    result_lines = line_backward(
        lines, grad_lines.reshape(lines.shape), gain_x, full_in_x, full_out_x
    )
    return lax.all_to_all(result_lines, "tr", split_axis=2, concat_axis=1, tiled=True)


def solution(mesh):
    return jax.shard_map(
        per_device,
        mesh=mesh,
        in_specs=(
            P("gz", None, "tr", None),
            P("gz", None, "tr", None),
            P(),
            P("tr", None),
            P("tr", None),
            P(),
            P("tr", None),
            P("tr", None),
        ),
        out_specs=P("gz", None, "tr", None),
        check_vma=False,
    )
```

profile of v0, /device:TPU:0, one launch (start us, length us, event | category | flops | bytes accessed | tf_op | source)
XLA Modules:
  0.0 194.4 jit_solution(14103475853062895245)
XLA Ops:
  10.5 4.2 %all-to-all-start.2 = ((bf16[5,32,2,768]{3,2,0,1:T(2,128)(2,1)}), bf16[5,32,2,768]{3,2,0,1:T(2,128)(2,1)S(1)}, u32[]{:S(2)}, u32[]{:S(2)}) async-start(bf16[5,32,2,768]{3,2,0,1:T(2,128)(2,1)} %copy.114), calls=%async_computation.2 | async-start | bytes 983040 | tf_op jit(solution)/shard_map/all_to_all | solution.py:114
  15.8 9.2 %all-to-all-done.2 = bf16[5,32,2,768]{3,2,0,1:T(2,128)(2,1)S(1)} async-done(((bf16[5,32,2,768]{3,2,0,1:T(2,128)(2,1)}), bf16[5,32,2,768]{3,2,0,1:T(2,128)(2,1)S(1)}, u32[]{:S(2)}, u32[]{:S(2)}) %all-to-all-start.2) | async-done | bytes 491552 | tf_op jit(solution)/shard_map/all_to_all | solution.py:114
  25.0 3.5 %all-to-all-start = ((bf16[5,32,2,768]{3,2,0,1:T(2,128)(2,1)}), bf16[5,32,2,768]{3,2,0,1:T(2,128)(2,1)S(1)}, u32[]{:S(2)}, u32[]{:S(2)}) async-start(bf16[5,32,2,768]{3,2,0,1:T(2,128)(2,1)} %copy.109), calls=%async_computation | async-start | bytes 983040 | tf_op jit(solution)/shard_map/all_to_all | solution.py:115
  29.4 13.1 %all-to-all-done = bf16[5,32,2,768]{3,2,0,1:T(2,128)(2,1)S(1)} async-done(((bf16[5,32,2,768]{3,2,0,1:T(2,128)(2,1)}), bf16[5,32,2,768]{3,2,0,1:T(2,128)(2,1)S(1)}, u32[]{:S(2)}, u32[]{:S(2)}) %all-to-all-start) | async-done | bytes 491552 | tf_op jit(solution)/shard_map/all_to_all | solution.py:115
  43.5 7.3 %all-to-all-start.1 = ((bf16[5,64,768]{2,0,1:T(8,128)(2,1)}), bf16[5,64,768]{2,0,1:T(8,128)(2,1)S(1)}, u32[]{:S(2)}, u32[]{:S(2)}) async-start(bf16[5,64,768]{2,0,1:T(8,128)(2,1)} %bitcast.2), calls=%async_computation.1 | async-start | bytes 1572864 | tf_op jit(solution)/shard_map/all_to_all | solution.py:118
  51.9 3.4 %convolution_convert_fusion.1 = bf16[40,8,2304]{2,1,0:T(8,128)(2,1)S(1)} fusion(bf16[768,2304]{1,0:T(8,128)(2,1)} %all-gather.5.cloned.1.call-done, f32[40,8,768]{2,1,0:T(8,128)S(1)} %reshape.140, f32[768]{0:T(1024)S(1)} %copy-done.8, f32[40,8]{1,0:T(8,128)S(1)} %copy.119), kind=kOutput, calls=%fused_computation.5 | convolution fusion | flops 1133936640 | bytes 6000896 | tf_op jit(solution)/shard_map/dot_general | solution.py:25
  57.1 11.9 %all-gather.7.cloned.1.call-done = bf16[768,768]{1,0:T(8,128)(2,1)} async-done(((bf16[192,768]{1,0:T(8,128)(2,1)}), bf16[768,768]{1,0:T(8,128)(2,1)}) %all-gather.7.cloned.1.call-update) | async-done | bytes 1179664 | tf_op jit(solution)/shard_map/all_gather | solution.py:107
  69.0 2.6 %fusion.40 = bf16[40,8,768]{2,1,0:T(8,128)(2,1)S(1)} fusion(f32[40,8,768]{2,1,0:T(8,128)S(1)} %reshape.140, bf16[768,768]{1,0:T(8,128)(2,1)} %all-gather.7.cloned.1.call-done, bf16[40,8,2304]{2,1,0:T(8,128)(2,1)} %copy-done.5, f32[40,6,8,8]{2,3,1,0:T(8,128)} %get-tuple-element.9, f32[40,6,8]{2,1,0:T(8,128)S(1)} %get-tuple-element.8), kind=kOutput, calls=%fused_computation.38 | convolution fusion | flops 382187520 | bytes 4136448 | tf_op jit(solution)/shard_map/dot_general | solution.py:54
  72.9 5.5 %all-to-all-start.3 = ((bf16[5,64,768]{2,0,1:T(8,128)(2,1)}), bf16[5,64,768]{2,0,1:T(8,128)(2,1)S(1)}, u32[]{:S(2)}, u32[]{:S(2)}) async-start(bf16[5,64,768]{2,0,1:T(8,128)(2,1)} %copy.121), calls=%async_computation.3 | async-start | bytes 1572864 | tf_op jit(solution)/shard_map/all_to_all | solution.py:122
  78.5 9.5 %all-gather.11.cloned.1.call-done = bf16[768,768]{1,0:T(8,128)(2,1)} async-done(((bf16[192,768]{1,0:T(8,128)(2,1)}), bf16[768,768]{1,0:T(8,128)(2,1)}) %all-gather.11.cloned.1.call-update) | async-done | bytes 1179664 | tf_op jit(solution)/shard_map/all_gather | solution.py:111
  88.1 2.6 %fusion.43 = bf16[40,8,6,128]{3,1,2,0:T(8,128)(2,1)} fusion(bf16[40,8,768]{2,1,0:T(8,128)(2,1)S(1)} %bitcast.138, bf16[768,768]{1,0:T(8,128)(2,1)} %all-gather.11.cloned.1.call-done), kind=kOutput, calls=%fused_computation.50 | convolution fusion | flops 377733120 | bytes 2162688 | tf_op jit(solution)/shard_map/dot_general | solution.py:64
  90.7 8.3 %all-to-all-done.3 = bf16[5,64,768]{2,0,1:T(8,128)(2,1)S(1)} async-done(((bf16[5,64,768]{2,0,1:T(8,128)(2,1)}), bf16[5,64,768]{2,0,1:T(8,128)(2,1)S(1)}, u32[]{:S(2)}, u32[]{:S(2)}) %all-to-all-start.3) | async-done | bytes 491552 | tf_op jit(solution)/shard_map/all_to_all | solution.py:122
  99.6 20.7 %all-gather.9.cloned.1.call-done = bf16[768,2304]{1,0:T(8,128)(2,1)} async-done(((bf16[192,2304]{1,0:T(8,128)(2,1)}), bf16[768,2304]{1,0:T(8,128)(2,1)}) %all-gather.9.cloned.1.call-update) | async-done | bytes 3538960 | tf_op jit(solution)/shard_map/all_gather | solution.py:110
  120.3 3.3 %convolution_convert_fusion = bf16[40,8,2304]{2,1,0:T(8,128)(2,1)S(1)} fusion(bf16[768,2304]{1,0:T(8,128)(2,1)} %all-gather.9.cloned.1.call-done, f32[40,8,768]{2,1,0:T(8,128)S(1)} %bitcast.135, f32[768]{0:T(1024)S(1)} %copy-done.7, f32[40,8]{1,0:T(8,128)S(1)} %reshape.158), kind=kOutput, calls=%fused_computation.4 | convolution fusion | flops 1133936640 | bytes 6000896 | tf_op jit(solution)/shard_map/dot_general | solution.py:25
  125.2 2.6 %fusion.106 = (f32[8,6,40]{2,1,0:T(8,128)S(1)}, f32[8,6,40,40]{2,3,1,0:T(8,128)}) fusion(bf16[40,8,6,128]{3,1,2,0:T(8,128)(2,1)S(1)} %get-tuple-element.7, bf16[40,8,6,128]{3,1,2,0:T(8,128)(2,1)} %get-tuple-element.6), kind=kOutput, calls=%fused_computation.123 | convolution fusion | flops 19891240 | bytes 1297920 | tf_op jit(solution)/shard_map/sub | solution.py:40
  127.8 2.6 %fusion.48 = bf16[40,8,6,128]{3,0,2,1:T(8,128)(2,1)} fusion(bf16[40,8,6,128]{3,1,2,0:T(8,128)(2,1)} %fusion.43, f32[8,6,40,40]{2,3,1,0:T(8,128)} %get-tuple-element.11, f32[8,6,40]{2,1,0:T(8,128)S(1)} %get-tuple-element.10), kind=kOutput, calls=%fused_computation.55 | convolution fusion | flops 20060160 | bytes 1297920 | tf_op jit(solution)/shard_map/bhlm,lbhe->mbhe/dot_general | solution.py:69
  130.3 3.0 %fusion.47 = bf16[40,8,6,128]{3,0,2,1:T(8,128)(2,1)} fusion(f32[8,6,40,40]{2,3,1,0:T(8,128)S(1)} %fusion.60, bf16[40,8,6,128]{3,1,2,0:T(8,128)(2,1)} %get-tuple-element.6, f32[8,6,40,40]{2,3,1,0:T(8,128)} %get-tuple-element.11, f32[8,6,40]{2,1,0:T(8,128)S(1)} %get-tuple-element.10), kind=kOutput, calls=%fused_computation.54 | convolution fusion | flops 20446120 | bytes 1605120 | tf_op jit(solution)/shard_map/bhlm,lbhe->mbhe/dot_general | solution.py:77
  133.3 2.9 %fusion.46 = bf16[40,8,6,128]{3,0,2,1:T(8,128)(2,1)} fusion(f32[8,6,40,40]{2,3,1,0:T(8,128)S(1)} %fusion.60, bf16[40,8,6,128]{3,1,2,0:T(8,128)(2,1)S(1)} %get-tuple-element.7, f32[8,6,40,40]{2,3,1,0:T(8,128)} %get-tuple-element.11, f32[8,6,40]{2,1,0:T(8,128)S(1)} %get-tuple-element.10), kind=kOutput, calls=%fused_computation.53 | convolution fusion | flops 20446120 | bytes 1605120 | tf_op jit(solution)/shard_map/bhlm,mbhe->lbhe/dot_general | solution.py:74
  138.8 3.5 %multiply_reduce_fusion.3 = (f32[40,8]{1,0:T(8,128)S(1)}, f32[40,8,768]{2,1,0:T(8,128)S(1)}) fusion(f32[40,8,768]{2,1,0:T(8,128)S(1)} %bitcast.136, f32[768]{0:T(1024)S(1)} %copy-done.7, bf16[768,2304]{1,0:T(8,128)(2,1)} %all-gather.9.cloned.1.call-done, bf16[40,8,768]{2,1,0:T(8,128)(2,1)S(1)} %get-tuple-element.16, ...), kind=kOutput, calls=%fused_computation.69 | convolution fusion | flops 1137622784 | bytes 6983936 | tf_op jit(solution)/shard_map/dot_general | solution.py:83
  142.6 19.6 %all_to_all.84 = bf16[40,8,768]{2,1,0:T(8,128)(2,1)S(1)} all-to-all(bf16[40,8,768]{2,1,0:T(8,128)(2,1)S(1)} %add_convert_fusion.1), channel_id=1, replica_groups=mesh['tr'=4,'gz'=8] {'gz'}, dimensions={0} | all-to-all | bytes 983040 | tf_op jit(solution)/shard_map/all_to_all | solution.py:126
  166.2 2.7 %fusion.49 = bf16[40,8,768]{2,1,0:T(8,128)(2,1)} fusion(f32[40,6,8,8]{2,3,1,0:T(8,128)S(1)} %fusion.79, bf16[40,8,2304]{2,1,0:T(8,128)(2,1)} %copy-done.5, f32[40,6,8,8]{2,3,1,0:T(8,128)S(1)} %copy-done.10, f32[40,6,8]{2,1,0:T(8,128)} %copy-done.11), kind=kOutput, calls=%fused_computation.56 | convolution fusion | flops 4287367 | bytes 5242880 | tf_op jit(solution)/shard_map/bhlm,bmhe->blhe/dot_general | solution.py:74
  168.9 2.6 %fusion.50 = bf16[40,8,768]{2,1,0:T(8,128)(2,1)} fusion(f32[40,6,8,8]{2,3,1,0:T(8,128)S(1)} %fusion.79, bf16[40,8,2304]{2,1,0:T(8,128)(2,1)} %copy-done.5, f32[40,6,8,8]{2,3,1,0:T(8,128)S(1)} %copy-done.10, f32[40,6,8]{2,1,0:T(8,128)} %copy-done.11), kind=kOutput, calls=%fused_computation.57 | convolution fusion | flops 4287367 | bytes 5242880 | tf_op jit(solution)/shard_map/bhlm,blhe->bmhe/dot_general | solution.py:77
  171.5 3.9 %multiply_reduce_fusion.2 = (f32[40,8]{1,0:T(8,128)S(1)}, f32[40,8,768]{2,1,0:T(8,128)S(1)}) fusion(f32[40,8,768]{2,1,0:T(8,128)S(1)} %reshape.140, f32[768]{0:T(1024)S(1)} %copy-done.8, bf16[768,2304]{1,0:T(8,128)(2,1)} %all-gather.5.cloned.1.call-done, bf16[40,8,768]{2,1,0:T(8,128)(2,1)} %fusion.51, bf16[40,8,768]{2,1,0:T(8,128)(2,1)} %fusion.50, ...), kind=kOutput, calls=%fused_computation.67 | convolution fusion | flops 1137622784 | bytes 6983936 | tf_op jit(solution)/shard_map/dot_general | solution.py:83
  175.9 10.9 %all_to_all.85 = bf16[5,8,8,768]{3,1,0,2:T(8,128)(2,1)S(1)} all-to-all(bf16[5,8,8,768]{3,1,0,2:T(8,128)(2,1)S(1)} %copy.139), channel_id=1, replica_groups=mesh['tr'=4,'gz'=8] {'tr'}, dimensions={2} | all-to-all | bytes 983040 | tf_op jit(solution)/shard_map/all_to_all | solution.py:130
  (71 shorter events, 21.5 us)
Async XLA Ops:
  6.5 2.8 %copy-start.2 = (bf16[5,32,2,768]{3,2,1,0:T(2,128)(2,1)S(1)}, bf16[5,32,2,768]{3,2,1,0:T(2,128)(2,1)}, u32[]{:S(2)}) copy-start(bf16[5,32,2,768]{3,2,1,0:T(2,128)(2,1)} %param.8) | copy-start | bytes 1474564
  6.5 45.4 %all-gather.5.cloned.1.call-start = ((), (), s32[]{:S(2)}) async-start(), calls=%async_computation.6 | async-start | bytes 4423680 | tf_op jit(solution)/shard_map/all_gather | solution.py:106
  7.3 61.8 %all-gather.7.cloned.1.call-start = ((), (), s32[]{:S(2)}) async-start(), calls=%async_computation.7 | async-start | bytes 1474560 | tf_op jit(solution)/shard_map/all_gather | solution.py:107
  8.0 80.1 %all-gather.11.cloned.1.call-start = ((), (), s32[]{:S(2)}) async-start(), calls=%async_computation.9 | async-start | bytes 1474560 | tf_op jit(solution)/shard_map/all_gather | solution.py:111
  8.7 5.9 %copy-start.3 = (bf16[5,32,2,768]{3,2,1,0:T(2,128)(2,1)S(1)}, bf16[5,32,2,768]{3,2,1,0:T(2,128)(2,1)}, u32[]{:S(2)}) copy-start(bf16[5,32,2,768]{3,2,1,0:T(2,128)(2,1)} %param.9) | copy-start | bytes 1474564
  8.8 111.5 %all-gather.9.cloned.1.call-start = ((), (), s32[]{:S(2)}) async-start(), calls=%async_computation.8 | async-start | bytes 4423680 | tf_op jit(solution)/shard_map/all_gather | solution.py:110
  10.5 14.5 %all-to-all-start.2 = ((bf16[5,32,2,768]{3,2,0,1:T(2,128)(2,1)}), bf16[5,32,2,768]{3,2,0,1:T(2,128)(2,1)S(1)}, u32[]{:S(2)}, u32[]{:S(2)}) async-start(bf16[5,32,2,768]{3,2,0,1:T(2,128)(2,1)} %copy.114), calls=%async_computation.2 | async-start | bytes 983040 | tf_op jit(solution)/shard_map/all_to_all | solution.py:114
  25.0 17.5 %all-to-all-start = ((bf16[5,32,2,768]{3,2,0,1:T(2,128)(2,1)}), bf16[5,32,2,768]{3,2,0,1:T(2,128)(2,1)S(1)}, u32[]{:S(2)}, u32[]{:S(2)}) async-start(bf16[5,32,2,768]{3,2,0,1:T(2,128)(2,1)} %copy.109), calls=%async_computation | async-start | bytes 983040 | tf_op jit(solution)/shard_map/all_to_all | solution.py:115
  43.5 29.4 %all-to-all-start.1 = ((bf16[5,64,768]{2,0,1:T(8,128)(2,1)}), bf16[5,64,768]{2,0,1:T(8,128)(2,1)S(1)}, u32[]{:S(2)}, u32[]{:S(2)}) async-start(bf16[5,64,768]{2,0,1:T(8,128)(2,1)} %bitcast.2), calls=%async_computation.1 | async-start | bytes 1572864 | tf_op jit(solution)/shard_map/all_to_all | solution.py:118
  50.8 1.1 copy-start.8
  55.3 1.8 copy-start.5
  57.1 14.6 %copy-start.11 = (f32[40,6,8]{2,1,0:T(8,128)}, f32[40,6,8]{2,1,0:T(8,128)S(1)}, u32[]{:S(2)}) copy-start(f32[40,6,8]{2,1,0:T(8,128)S(1)} %get-tuple-element.8) | copy-start | bytes 23044
  72.9 26.1 %all-to-all-start.3 = ((bf16[5,64,768]{2,0,1:T(8,128)(2,1)}), bf16[5,64,768]{2,0,1:T(8,128)(2,1)S(1)}, u32[]{:S(2)}, u32[]{:S(2)}) async-start(bf16[5,64,768]{2,0,1:T(8,128)(2,1)} %copy.121), calls=%async_computation.3 | async-start | bytes 1572864 | tf_op jit(solution)/shard_map/all_to_all | solution.py:122
  78.5 20.7 %copy-start = (bf16[8,5,8,768]{3,2,1,0:T(8,128)(2,1)}, bf16[8,5,8,768]{3,2,1,0:T(8,128)(2,1)S(1)}, u32[]{:S(2)}) copy-start(bf16[8,5,8,768]{3,2,1,0:T(8,128)(2,1)S(1)} %copy.113) | copy-start | bytes 1474564
  90.7 29.6 %copy-start.7 = (f32[768]{0:T(1024)S(1)}, f32[768]{0:T(1024)}, u32[]{:S(2)}) copy-start(f32[768]{0:T(1024)} %param.13) | copy-start | bytes 9220
  123.7 1.1 copy-start.4
  138.8 3.5 %copy-start.1 = (bf16[8,5,8,768]{3,2,1,0:T(8,128)(2,1)S(1)}, bf16[8,5,8,768]{3,2,1,0:T(8,128)(2,1)}, u32[]{:S(2)}) copy-start(bf16[8,5,8,768]{3,2,1,0:T(8,128)(2,1)} %copy-done) | copy-start | bytes 1474564
  142.6 19.7 %copy-start.6 = (bf16[768,768]{1,0:T(8,128)(2,1)S(1)}, bf16[768,768]{1,0:T(8,128)(2,1)}, u32[]{:S(2)}) copy-start(bf16[768,768]{1,0:T(8,128)(2,1)} %all-gather.7.cloned.1.call-done) | copy-start | bytes 3538948
  162.3 1.2 copy-start.9
  162.3 1.2 copy-start.12
  164.7 1.5 copy-start.10
Sparse Core Ops, SparseCore 0:
  8.9 40.0 all-gather.4
  50.5 18.4 all-gather.6
  70.6 17.4 all-gather.10
  89.5 30.7 all-gather.8
where the time goes:
time: 195 us; the launch traced here: 194 us
  waiting for transfers between devices  75.3 us (39%)
  matrix products  41.2 us (21%)
  blocking collectives  30.5 us (16%)
  starting transfers between devices  20.6 us (11%)
  between operations  13.4 us (7%)
  local copies, waits for them, and re-layouts  11.4 us (6%)
    all_gather x1, waiting for transfers between devices, per_device(): lax.all_gather(wqkv_z, 'tr', axis=0, tiled=True)  20.7 us
    all_to_all x1, blocking collectives, per_device(): lax.all_to_all(grad_columns, 'gz', split_axis=0, concat_axis=1, tiled=True)  19.6 us
    all_to_all x1, waiting for transfers between devices, per_device(): lax.all_to_all(cotangent, 'tr', split_axis=1, concat_axis=2, tiled=True)  13.1 us
    all_gather x1, waiting for transfers between devices, per_device(): lax.all_gather(wo_x, 'tr', axis=0, tiled=True)  11.9 us
    all_to_all x1, blocking collectives, per_device(): lax.all_to_all(result_lines, 'tr', split_axis=2, concat_axis=1, tiled=True)  10.9 us
    all_gather x1, waiting for transfers between devices, per_device(): lax.all_gather(wo_z, 'tr', axis=0, tiled=True)  9.53 us
    all_to_all x1, waiting for transfers between devices, per_device(): lax.all_to_all(tokens, 'tr', split_axis=1, concat_axis=2, tiled=True)  9.19 us
    all_to_all x1, waiting for transfers between devices, per_device(): lax.all_to_all(mid_lines.reshape(flat), 'gz', split_axis=1, concat_axis=0...  8.26 us
  transfers between devices with their start and end apart: 8, of which 6 were waited for; matrix products, arithmetic and copies ran while one was open for 9% of the time, Pallas kernels for 0%

commit v1 on v0

--- a/solution.py
+++ b/solution.py
@@ -5,6 +5,18 @@
 from jax.sharding import PartitionSpec as P
 
 H = 6
+
+
+def gather_by_bits(x, axis, dim):
+    ways, here, hop = (lax.axis_size(axis), lax.axis_index(axis), x.shape[dim])
+    line, have = (x, 1)
+    while have < ways:
+        line = jnp.concatenate(
+            [line, lax.ppermute(line, axis, [(d, (d - have) % ways) for d in range(ways)])],
+            axis=dim,
+        )
+        have = 2 * have
+    return jnp.roll(line, here * hop, axis=dim)
 
 
 def head_split(packed, index, model_width):
@@ -104,7 +116,7 @@
 def per_device(tokens, cotangent, gain_x, wqkv_x, wo_x, gain_z, wqkv_z, wo_z):
     full_in_x, full_out_x = (
         lax.all_gather(wqkv_x, "tr", axis=0, tiled=True),
-        lax.all_gather(wo_x, "tr", axis=0, tiled=True),
+        gather_by_bits(wo_x, "tr", 0),
     )
     full_in_z, full_out_z = (
         lax.all_gather(wqkv_z, "tr", axis=0, tiled=True),

time: 195 us -> 189 us (0.969)
  waiting for transfers between devices: 75.3 us -> 58.9 us
  local copies, waits for them, and re-layouts: 11.4 us -> 18.3 us
    all_gather x1, waiting for transfers between devices: 20.7 us -> 0.44 us  [per_device(): lax.all_gather(wqkv_z, 'tr', axis=0, tiled=True)]
    all_to_all x1, waiting for transfers between devices: 13.1 us -> 28.6 us  [per_device(): lax.all_to_all(cotangent, 'tr', split_axis=1, concat_axis=2, tiled=True)]
    all_gather x1 -> x0, waiting for transfers between devices: 11.9 us -> none  [per_device(): lax.all_gather(wo_x, 'tr', axis=0, tiled=True)]
    all_gather x1, waiting for transfers between devices: 9.53 us -> 0.02 us  [per_device(): lax.all_gather(wo_z, 'tr', axis=0, tiled=True)]
    all_to_all x1, waiting for transfers between devices: 8.26 us -> 17.2 us  [per_device(): lax.all_to_all(mid_lines.reshape(flat), 'gz', split_axis=1, concat_axis=0...]
    all_to_all x1, waiting for transfers between devices: 0.01 us -> 4.43 us  [per_device(): lax.all_to_all(cot_lines.reshape(flat), 'gz', split_axis=1, concat_axis=0...]
    ppermute x0 -> x2, starting transfers between devices: none -> 4.39 us  [gather_by_bits(): lax.ppermute(line, axis, [(d, (d - have) % ways) for d in range(ways)])]
    unnamed x28 -> x33, local copies, waits for them, and re-layouts: 3.01 us -> 7.26 us
  transfers between devices with their start and end apart: 8 -> 9, of which waited for: 6 -> 5; matrix products, arithmetic and copies ran while one was open for 9% -> 14% of each run, Pallas kernels for 0% -> 0%
where the time goes in v1:
time: 189 us; the launch traced here: 188 us
  waiting for transfers between devices  58.9 us (31%)
  matrix products  43.1 us (23%)
  blocking collectives  30.5 us (16%)
  starting transfers between devices  21 us (11%)
  local copies, waits for them, and re-layouts  18.3 us (10%)
  between operations  13.5 us (7%)
  other arithmetic  2.79 us (1%)
    all_to_all x1, waiting for transfers between devices, per_device(): lax.all_to_all(cotangent, 'tr', split_axis=1, concat_axis=2, tiled=True)  28.6 us
    all_to_all x1, blocking collectives, per_device(): lax.all_to_all(grad_columns, 'gz', split_axis=0, concat_axis=1, tiled=True)  19.6 us
    all_to_all x1, waiting for transfers between devices, per_device(): lax.all_to_all(mid_lines.reshape(flat), 'gz', split_axis=1, concat_axis=0...  17.2 us
    all_to_all x1, blocking collectives, per_device(): lax.all_to_all(result_lines, 'tr', split_axis=2, concat_axis=1, tiled=True)  10.9 us
    unnamed x33, local copies, waits for them, and re-layouts  7.26 us
    dot_general x2, matrix products, backward(): d_normed = jnp.dot(joined, w_in.T, preferred_element_type=jnp.float32)  7.23 us
    dot_general x2, matrix products, recompute(): jnp.dot(normed, w_in, preferred_element_type=jnp.float32)  6.73 us
    dot_general x2, matrix products, backward(): jnp.einsum('bhlm,' + key_form + '->' + layout, d_scores, key_part, prefer...  6.3 us
  transfers between devices with their start and end apart: 9, of which 5 were waited for; matrix products, arithmetic and copies ran while one was open for 14% of the time, Pallas kernels for 0%

profile of v1, /device:TPU:0, one launch (start us, length us, event | category | flops | bytes accessed | tf_op | source)
XLA Modules:
  0.0 188.1 jit_solution(11789087588935349731)
XLA Ops:
  8.7 2.4 %collective-permute-start = (bf16[192,768]{1,0:T(8,128)(2,1)}, bf16[192,768]{1,0:T(8,128)(2,1)S(1)}, u32[]{:S(2)}, u32[]{:S(2)}) collective-permute-start(bf16[192,768]{1,0:T(8,128)(2,1)} %param.12), channel_id=1, source_target_pairs={{0,24},{8,0},{16,8},{24,16},{1,25},{9,1},{17,9},{25,17},{2,26},{10... | collective-permute-start | bytes 884744 | tf_op jit(solution)/shard_map/ppermute | solution.py:15
  12.3 3.5 %all-to-all-start.2 = ((bf16[5,32,2,768]{3,2,0,1:T(2,128)(2,1)}), bf16[5,32,2,768]{3,2,0,1:T(2,128)(2,1)S(1)}, u32[]{:S(2)}, u32[]{:S(2)}) async-start(bf16[5,32,2,768]{3,2,0,1:T(2,128)(2,1)} %copy.114), calls=%async_computation.2 | async-start | bytes 983040 | tf_op jit(solution)/shard_map/all_to_all | solution.py:126
  21.3 6.1 %all-to-all-done.2 = bf16[5,32,2,768]{3,2,0,1:T(2,128)(2,1)S(1)} async-done(((bf16[5,32,2,768]{3,2,0,1:T(2,128)(2,1)}), bf16[5,32,2,768]{3,2,0,1:T(2,128)(2,1)S(1)}, u32[]{:S(2)}, u32[]{:S(2)}) %all-to-all-start.2) | async-done | bytes 491552 | tf_op jit(solution)/shard_map/all_to_all | solution.py:126
  27.4 3.5 %all-to-all-start = ((bf16[5,32,2,768]{3,2,0,1:T(2,128)(2,1)}), bf16[5,32,2,768]{3,2,0,1:T(2,128)(2,1)S(1)}, u32[]{:S(2)}, u32[]{:S(2)}) async-start(bf16[5,32,2,768]{3,2,0,1:T(2,128)(2,1)} %copy.109), calls=%async_computation | async-start | bytes 983040 | tf_op jit(solution)/shard_map/all_to_all | solution.py:127
  32.5 28.6 %all-to-all-done = bf16[5,32,2,768]{3,2,0,1:T(2,128)(2,1)S(1)} async-done(((bf16[5,32,2,768]{3,2,0,1:T(2,128)(2,1)}), bf16[5,32,2,768]{3,2,0,1:T(2,128)(2,1)S(1)}, u32[]{:S(2)}, u32[]{:S(2)}) %all-to-all-start) | async-done | bytes 491552 | tf_op jit(solution)/shard_map/all_to_all | solution.py:127
  62.1 5.8 %all-to-all-start.1 = ((bf16[5,64,768]{2,0,1:T(8,128)(2,1)}), bf16[5,64,768]{2,0,1:T(8,128)(2,1)S(1)}, u32[]{:S(2)}, u32[]{:S(2)}) async-start(bf16[5,64,768]{2,0,1:T(8,128)(2,1)} %bitcast.2), calls=%async_computation.1 | async-start | bytes 1572864 | tf_op jit(solution)/shard_map/all_to_all | solution.py:130
  72.5 2.0 %constant_dynamic-update-slice_fusion = bf16[1536,768]{1,0:T(8,128)(2,1)} fusion(bf16[1536,768]{1,0:T(8,128)(2,1)} %constant_dynamic-update-slice_fusion.1, bf16[384,768]{1,0:T(8,128)(2,1)} %collective-permute-done.1), kind=kLoop, calls=%fused_computation.108 | loop fusion | bytes 1179648 | tf_op jit(solution)/shard_map/jit(_roll_dynamic)/concatenate | solution.py:19
  74.5 3.4 %convolution_convert_fusion.1 = bf16[40,8,2304]{2,1,0:T(8,128)(2,1)S(1)} fusion(bf16[768,2304]{1,0:T(8,128)(2,1)} %all-gather.4.cloned.1.call-done, f32[40,8,768]{2,1,0:T(8,128)S(1)} %reshape.140, f32[768]{0:T(1024)S(1)} %copy-done.11, f32[40,8]{1,0:T(8,128)} %copy.119), kind=kOutput, calls=%fused_computation.5 | convolution fusion | flops 1133936640 | bytes 6000896 | tf_op jit(solution)/shard_map/dot_general | solution.py:37
  79.7 2.7 %fusion.40 = bf16[40,8,768]{2,1,0:T(8,128)(2,1)S(1)} fusion(f32[40,8,768]{2,1,0:T(8,128)S(1)} %reshape.140, bf16[1536,768]{1,0:T(8,128)(2,1)} %constant_dynamic-update-slice_fusion, s32[]{:T(128)S(6)} %select_n.14, bf16[40,8,2304]{2,1,0:T(8,128)(2,1)} %copy-done.8, f32[40,6,8,8]{2,3,1,0:T(8,128)} %get-tuple-element.9, f32[40,6,8]{2,1,0:T(8,128)S(1)} %get-tuple-element.8), kind=kOutput, calls=%fused_computation.38 | convolution fusion | flops 382187520 | bytes 4136452 | tf_op jit(solution)/shard_map/dot_general | solution.py:66
  83.6 4.4 %all-to-all-done.1 = bf16[5,64,768]{2,0,1:T(8,128)(2,1)S(1)} async-done(((bf16[5,64,768]{2,0,1:T(8,128)(2,1)}), bf16[5,64,768]{2,0,1:T(8,128)(2,1)S(1)}, u32[]{:S(2)}, u32[]{:S(2)}) %all-to-all-start.1) | async-done | bytes 491552 | tf_op jit(solution)/shard_map/all_to_all | solution.py:130
  88.0 3.7 %all-to-all-start.3 = ((bf16[5,64,768]{2,0,1:T(8,128)(2,1)}), bf16[5,64,768]{2,0,1:T(8,128)(2,1)S(1)}, u32[]{:S(2)}, u32[]{:S(2)}) async-start(bf16[5,64,768]{2,0,1:T(8,128)(2,1)} %copy.121), calls=%async_computation.3 | async-start | bytes 1572864 | tf_op jit(solution)/shard_map/all_to_all | solution.py:134
  91.9 2.8 %fusion.43 = bf16[40,8,6,128]{3,1,2,0:T(8,128)(2,1)} fusion(bf16[40,8,768]{2,1,0:T(8,128)(2,1)S(1)} %bitcast.138, bf16[768,768]{1,0:T(8,128)(2,1)} %all-gather.8.cloned.1.call-done), kind=kOutput, calls=%fused_computation.50 | convolution fusion | flops 377733120 | bytes 2162688 | tf_op jit(solution)/shard_map/dot_general | solution.py:76
  94.7 17.2 %all-to-all-done.3 = bf16[5,64,768]{2,0,1:T(8,128)(2,1)S(1)} async-done(((bf16[5,64,768]{2,0,1:T(8,128)(2,1)}), bf16[5,64,768]{2,0,1:T(8,128)(2,1)S(1)}, u32[]{:S(2)}, u32[]{:S(2)}) %all-to-all-start.3) | async-done | bytes 491552 | tf_op jit(solution)/shard_map/all_to_all | solution.py:134
  112.9 3.3 %convolution_convert_fusion = bf16[40,8,2304]{2,1,0:T(8,128)(2,1)S(1)} fusion(bf16[768,2304]{1,0:T(8,128)(2,1)} %all-gather.6.cloned.1.call-done, f32[40,8,768]{2,1,0:T(8,128)S(1)} %bitcast.135, f32[768]{0:T(1024)S(1)} %copy-done.10, f32[40,8]{1,0:T(8,128)S(1)} %reshape.158), kind=kOutput, calls=%fused_computation.4 | convolution fusion | flops 1133936640 | bytes 6000896 | tf_op jit(solution)/shard_map/dot_general | solution.py:37
  117.8 2.8 %fusion.110 = (f32[8,6,40]{2,1,0:T(8,128)S(1)}, f32[8,6,40,40]{2,3,1,0:T(8,128)}) fusion(bf16[40,8,6,128]{3,1,2,0:T(8,128)(2,1)} %get-tuple-element.7, bf16[40,8,6,128]{3,1,2,0:T(8,128)(2,1)} %get-tuple-element.6), kind=kOutput, calls=%fused_computation.134 | convolution fusion | flops 19891240 | bytes 1297920 | tf_op jit(solution)/shard_map/sub | solution.py:52
  120.6 2.6 %fusion.48 = bf16[40,8,6,128]{3,0,2,1:T(8,128)(2,1)} fusion(bf16[40,8,6,128]{3,1,2,0:T(8,128)(2,1)} %fusion.43, f32[8,6,40,40]{2,3,1,0:T(8,128)} %get-tuple-element.11, f32[8,6,40]{2,1,0:T(8,128)S(1)} %get-tuple-element.10), kind=kOutput, calls=%fused_computation.55 | convolution fusion | flops 20060160 | bytes 1297920 | tf_op jit(solution)/shard_map/bhlm,lbhe->mbhe/dot_general | solution.py:81
  123.1 3.0 %fusion.47 = bf16[40,8,6,128]{3,0,2,1:T(8,128)(2,1)} fusion(f32[8,6,40,40]{2,3,1,0:T(8,128)S(1)} %fusion.62, bf16[40,8,6,128]{3,1,2,0:T(8,128)(2,1)} %get-tuple-element.6, f32[8,6,40,40]{2,3,1,0:T(8,128)} %get-tuple-element.11, f32[8,6,40]{2,1,0:T(8,128)S(1)} %get-tuple-element.10), kind=kOutput, calls=%fused_computation.54 | convolution fusion | flops 20446120 | bytes 1605120 | tf_op jit(solution)/shard_map/bhlm,lbhe->mbhe/dot_general | solution.py:89
  126.1 3.1 %fusion.46 = bf16[40,8,6,128]{3,0,2,1:T(8,128)(2,1)} fusion(f32[8,6,40,40]{2,3,1,0:T(8,128)S(1)} %fusion.62, bf16[40,8,6,128]{3,1,2,0:T(8,128)(2,1)} %get-tuple-element.7, f32[8,6,40,40]{2,3,1,0:T(8,128)} %get-tuple-element.11, f32[8,6,40]{2,1,0:T(8,128)S(1)} %get-tuple-element.10), kind=kOutput, calls=%fused_computation.53 | convolution fusion | flops 20446120 | bytes 1605120 | tf_op jit(solution)/shard_map/bhlm,mbhe->lbhe/dot_general | solution.py:86
  131.7 3.5 %multiply_reduce_fusion.3 = (f32[40,8]{1,0:T(8,128)S(1)}, f32[40,8,768]{2,1,0:T(8,128)S(1)}) fusion(f32[40,8,768]{2,1,0:T(8,128)S(1)} %bitcast.136, f32[768]{0:T(1024)S(1)} %copy-done.10, bf16[768,2304]{1,0:T(8,128)(2,1)} %all-gather.6.cloned.1.call-done, bf16[40,8,768]{2,1,0:T(8,128)(2,1)S(1)} %get-tuple-element.16, ...), kind=kOutput, calls=%fused_computation.71 | convolution fusion | flops 1137622784 | bytes 6983936 | tf_op jit(solution)/shard_map/dot_general | solution.py:95
  135.5 19.6 %all_to_all.84 = bf16[40,8,768]{2,1,0:T(8,128)(2,1)S(1)} all-to-all(bf16[40,8,768]{2,1,0:T(8,128)(2,1)S(1)} %add_convert_fusion.1), channel_id=1, replica_groups=mesh['tr'=4,'gz'=8] {'gz'}, dimensions={0} | all-to-all | bytes 983040 | tf_op jit(solution)/shard_map/all_to_all | solution.py:138
  158.9 3.2 %fusion.49 = bf16[40,8,768]{2,1,0:T(8,128)(2,1)} fusion(f32[40,6,8,8]{2,3,1,0:T(8,128)S(1)} %fusion.81, bf16[40,8,2304]{2,1,0:T(8,128)(2,1)} %copy-done.8, f32[40,6,8,8]{2,3,1,0:T(8,128)} %get-tuple-element.9, f32[40,6,8]{2,1,0:T(8,128)S(1)} %get-tuple-element.8), kind=kOutput, calls=%fused_computation.56 | convolution fusion | flops 4287367 | bytes 4321280 | tf_op jit(solution)/shard_map/bhlm,bmhe->blhe/dot_general | solution.py:86
  162.2 3.2 %fusion.50 = bf16[40,8,768]{2,1,0:T(8,128)(2,1)} fusion(f32[40,6,8,8]{2,3,1,0:T(8,128)S(1)} %fusion.81, bf16[40,8,2304]{2,1,0:T(8,128)(2,1)} %copy-done.8, f32[40,6,8,8]{2,3,1,0:T(8,128)} %get-tuple-element.9, f32[40,6,8]{2,1,0:T(8,128)S(1)} %get-tuple-element.8), kind=kOutput, calls=%fused_computation.57 | convolution fusion | flops 4287367 | bytes 4321280 | tf_op jit(solution)/shard_map/bhlm,blhe->bmhe/dot_general | solution.py:89
  165.4 3.7 %multiply_reduce_fusion.2 = (f32[40,8]{1,0:T(8,128)S(1)}, f32[40,8,768]{2,1,0:T(8,128)S(1)}) fusion(f32[40,8,768]{2,1,0:T(8,128)S(1)} %reshape.140, f32[768]{0:T(1024)S(1)} %copy-done.11, bf16[768,2304]{1,0:T(8,128)(2,1)} %all-gather.4.cloned.1.call-done, bf16[40,8,768]{2,1,0:T(8,128)(2,1)S(1)} %fusion.51, bf16[40,8,768]{2,1,0:T(8,128)(2,1)} %fusion.50, ...), kind=kOutput, calls=%fused_computation.69 | convolution fusion | flops 1137622784 | bytes 6983936 | tf_op jit(solution)/shard_map/dot_general | solution.py:95
  169.6 10.9 %all_to_all.85 = bf16[5,8,8,768]{3,1,0,2:T(8,128)(2,1)S(1)} all-to-all(bf16[5,8,8,768]{3,1,0,2:T(8,128)(2,1)S(1)} %copy.139), channel_id=1, replica_groups=mesh['tr'=4,'gz'=8] {'tr'}, dimensions={2} | all-to-all | bytes 983040 | tf_op jit(solution)/shard_map/all_to_all | solution.py:142
  (79 shorter events, 29.6 us)
Async XLA Ops:
  6.5 10.4 %copy-start = (bf16[192,768]{1,0:T(8,128)(2,1)S(1)}, bf16[192,768]{1,0:T(8,128)(2,1)}, u32[]{:S(2)}) copy-start(bf16[192,768]{1,0:T(8,128)(2,1)} %param.12) | copy-start | bytes 884740
  6.5 4.6 %copy-start.5 = (bf16[5,32,2,768]{3,2,1,0:T(2,128)(2,1)S(1)}, bf16[5,32,2,768]{3,2,1,0:T(2,128)(2,1)}, u32[]{:S(2)}) copy-start(bf16[5,32,2,768]{3,2,1,0:T(2,128)(2,1)} %param.8) | copy-start | bytes 1474564
  6.5 9.3 %copy-start.6 = (bf16[5,32,2,768]{3,2,1,0:T(2,128)(2,1)S(1)}, bf16[5,32,2,768]{3,2,1,0:T(2,128)(2,1)}, u32[]{:S(2)}) copy-start(bf16[5,32,2,768]{3,2,1,0:T(2,128)(2,1)} %param.9) | copy-start | bytes 1474564
  6.5 68.0 %all-gather.4.cloned.1.call-start = ((), (), s32[]{:S(2)}) async-start(), calls=%async_computation.6 | async-start | bytes 4423680 | tf_op jit(solution)/shard_map/all_gather | solution.py:118
  7.3 84.6 %all-gather.8.cloned.1.call-start = ((), (), s32[]{:S(2)}) async-start(), calls=%async_computation.8 | async-start | bytes 1474560 | tf_op jit(solution)/shard_map/all_gather | solution.py:123
  8.0 104.9 %all-gather.6.cloned.1.call-start = ((), (), s32[]{:S(2)}) async-start(), calls=%async_computation.7 | async-start | bytes 4423680 | tf_op jit(solution)/shard_map/all_gather | solution.py:122
  8.7 8.9 %collective-permute-start = (bf16[192,768]{1,0:T(8,128)(2,1)}, bf16[192,768]{1,0:T(8,128)(2,1)S(1)}, u32[]{:S(2)}, u32[]{:S(2)}) collective-permute-start(bf16[192,768]{1,0:T(8,128)(2,1)} %param.12), channel_id=1, source_target_pairs={{0,24},{8,0},{16,8},{24,16},{1,25},{9,1},{17,9},{25,17},{2,26},{10... | collective-permute-start | bytes 884744 | tf_op jit(solution)/shard_map/ppermute | solution.py:15
  12.3 15.1 %all-to-all-start.2 = ((bf16[5,32,2,768]{3,2,0,1:T(2,128)(2,1)}), bf16[5,32,2,768]{3,2,0,1:T(2,128)(2,1)S(1)}, u32[]{:S(2)}, u32[]{:S(2)}) async-start(bf16[5,32,2,768]{3,2,0,1:T(2,128)(2,1)} %copy.114), calls=%async_computation.2 | async-start | bytes 983040 | tf_op jit(solution)/shard_map/all_to_all | solution.py:126
  17.7 44.5 %copy-start.1 = (bf16[192,768]{1,0:T(8,128)(2,1)}, bf16[192,768]{1,0:T(8,128)(2,1)S(1)}, u32[]{:S(2)}) copy-start(bf16[192,768]{1,0:T(8,128)(2,1)S(1)} %collective-permute-done) | copy-start | bytes 884740
  18.6 50.5 %collective-permute-start.1 = (bf16[384,768]{1,0:T(8,128)(2,1)}, bf16[384,768]{1,0:T(8,128)(2,1)}, u32[]{:S(2)}, u32[]{:S(2)}) collective-permute-start(bf16[384,768]{1,0:T(8,128)(2,1)} %pad_maximum_fusion), channel_id=1, source_target_pairs={{0,16},{8,24},{16,0},{24,8},{1,17},{9,25},{17,1},{25,9},{2,18},{10... | collective-permute-start | bytes 1769480 | tf_op jit(solution)/shard_map/ppermute | solution.py:15
  27.4 33.7 %all-to-all-start = ((bf16[5,32,2,768]{3,2,0,1:T(2,128)(2,1)}), bf16[5,32,2,768]{3,2,0,1:T(2,128)(2,1)S(1)}, u32[]{:S(2)}, u32[]{:S(2)}) async-start(bf16[5,32,2,768]{3,2,0,1:T(2,128)(2,1)} %copy.109), calls=%async_computation | async-start | bytes 983040 | tf_op jit(solution)/shard_map/all_to_all | solution.py:127
  62.1 25.9 %all-to-all-start.1 = ((bf16[5,64,768]{2,0,1:T(8,128)(2,1)}), bf16[5,64,768]{2,0,1:T(8,128)(2,1)S(1)}, u32[]{:S(2)}, u32[]{:S(2)}) async-start(bf16[5,64,768]{2,0,1:T(8,128)(2,1)} %bitcast.2), calls=%async_computation.1 | async-start | bytes 1572864 | tf_op jit(solution)/shard_map/all_to_all | solution.py:130
  68.3 3.4 %copy-start.2 = (bf16[192,768]{1,0:T(8,128)(2,1)S(1)}, bf16[192,768]{1,0:T(8,128)(2,1)}, u32[]{:S(2)}) copy-start(bf16[192,768]{1,0:T(8,128)(2,1)} %copy-done.1) | copy-start | bytes 884740
  68.3 6.2 %copy-start.11 = (f32[768]{0:T(1024)S(1)}, f32[768]{0:T(1024)}, u32[]{:S(2)}) copy-start(f32[768]{0:T(1024)} %param.10) | copy-start | bytes 9220
  77.9 1.8 copy-start.8
  88.0 23.9 %all-to-all-start.3 = ((bf16[5,64,768]{2,0,1:T(8,128)(2,1)}), bf16[5,64,768]{2,0,1:T(8,128)(2,1)S(1)}, u32[]{:S(2)}, u32[]{:S(2)}) async-start(bf16[5,64,768]{2,0,1:T(8,128)(2,1)} %copy.121), calls=%async_computation.3 | async-start | bytes 1572864 | tf_op jit(solution)/shard_map/all_to_all | solution.py:134
  91.9 20.5 %copy-start.3 = (bf16[8,5,8,768]{3,2,1,0:T(8,128)(2,1)}, bf16[8,5,8,768]{3,2,1,0:T(8,128)(2,1)S(1)}, u32[]{:S(2)}) copy-start(bf16[8,5,8,768]{3,2,1,0:T(8,128)(2,1)S(1)} %copy.113) | copy-start | bytes 1474564
  91.9 21.0 %copy-start.10 = (f32[768]{0:T(1024)S(1)}, f32[768]{0:T(1024)}, u32[]{:S(2)}) copy-start(f32[768]{0:T(1024)} %param.13) | copy-start | bytes 9220
  116.3 1.1 copy-start.7
  131.7 3.5 %copy-start.4 = (bf16[8,5,8,768]{3,2,1,0:T(8,128)(2,1)S(1)}, bf16[8,5,8,768]{3,2,1,0:T(8,128)(2,1)}, u32[]{:S(2)}) copy-start(bf16[8,5,8,768]{3,2,1,0:T(8,128)(2,1)} %copy-done.3) | copy-start | bytes 1474564
  135.5 21.6 %copy-start.12 = (f32[40,6,8,8]{2,3,1,0:T(8,128)S(1)}, f32[40,6,8,8]{2,3,1,0:T(8,128)}, u32[]{:S(2)}) copy-start(f32[40,6,8,8]{2,3,1,0:T(8,128)} %get-tuple-element.9) | copy-start | bytes 184324
  165.4 3.8 %copy-start.9 = (f32[40,8]{1,0:T(8,128)S(1)}, f32[40,8]{1,0:T(8,128)}, u32[]{:S(2)}) copy-start(f32[40,8]{1,0:T(8,128)} %copy.119) | copy-start | bytes 3844
Sparse Core Ops, SparseCore 0:
  8.9 52.5 all-gather.3
  63.1 17.4 all-gather.7
  82.1 30.7 all-gather.5
